TPU v7x, 256 devices: a whole 4x4x8 slice. The times are simulated.
256 devices in a mesh: ctx: 8 (over z_lo, core), tp: 32 (over z_hi, y, x).
Axes of the slice: x: 4, y: 4, z: 8 (z_hi: 2, z_lo: 4; z = z_hi * 4 + z_lo), core: 2. Of those that a mesh axis runs over, the one named last changes fastest.
Arguments:
- tokens: bfloat16 [4096, 8192], P('ctx', 'tp'), may hold values from -6 to 6
- w_in: bfloat16 [8192, 3, 8192], P('ctx', None, 'tp'), may hold values from -0.0625 to 0.0625
- short_taps: float32 [3, 3, 8192], P(None, None, 'tp'), may hold values from -3 to 3
- decay_rate: float32 [8192, 16], P('tp'), may hold values from 0.00012207031 to 0.05
- residue: float32 [8192, 16], P('tp'), may hold values from -1.5 to 1.5
- skip_gain: float32 [8192], P('tp'), may hold values from -4 to 4
- w_out: bfloat16 [8192, 8192], P(None, 'tp'), may hold values from -0.0625 to 0.0625
Outputs:
- mixed: bfloat16 [4096, 8192], P('ctx', 'tp')
All inputs are finite; a program needn't handle non-finite values.
Results may differ from a plain program's by a relative error of at most 0.007.
Values may be sent and summed in bfloat16 or wider, within the bound.
A program may use at most 128 MiB of HBM per device.

v0:
```python
import jax
import jax.numpy as jnp
from jax import lax
from jax.sharding import PartitionSpec as P

BLK = 128


HIGH = lax.Precision.HIGHEST


def shifted(array, axis, by):
    length = lax.axis_size(axis)
    pairs = [(i, i + by) for i in range(length) if 0 <= i + by < length]
    return lax.ppermute(array, axis, pairs)


def body(tokens, w_in, short_taps, decay_rate, residue, skip_gain, w_out):
    length = tokens.shape[0]
    chans = decay_rate.shape[0]
    modes = decay_rate.shape[1]
    blocks = length // BLK
    whole = lax.all_gather(tokens, "tp", axis=1, tiled=True)
    piece = lax.all_gather(w_in, "ctx", axis=0, tiled=True)
    summed = jnp.dot(
        whole, piece.reshape(piece.shape[0], 3 * chans), preferred_element_type=jnp.float32
    )
    proj = summed.astype(jnp.bfloat16).reshape(length, 3, chans)
    before = shifted(proj[-2:], "ctx", 1)
    extended = jnp.concatenate([before, proj], axis=0).astype(jnp.float32)
    feat = (
        short_taps[0] * extended[2:]
        + short_taps[1] * extended[1:-1]
        + short_taps[2] * extended[:-2]
    )
    query, keys, values = (feat[:, 0], feat[:, 1], feat[:, 2])
    drive = keys * values
    pole = jnp.exp(-decay_rate)
    weight = residue * jnp.sqrt(1.0 - pole * pole)
    steps = jnp.arange(BLK, dtype=jnp.float32)
    powers = jnp.exp(-decay_rate[:, :, None] * steps)
    lagged = jnp.sum(weight[:, :, None] * powers, axis=1)
    offset = jnp.arange(BLK)[:, None] - jnp.arange(BLK)[None, :]
    selector = (offset[None] == jnp.arange(BLK)[:, None, None]).astype(jnp.float32)
    toeplitz = jnp.einsum("ck,kij->cij", lagged, selector, precision=HIGH)
    split = drive.reshape(blocks, BLK, chans)
    local = jnp.einsum("bjc,cij->bic", split, toeplitz, precision=HIGH)
    ends = jnp.einsum("bjc,crj->bcr", split, powers[:, :, ::-1], precision=HIGH)
    index = jnp.arange(blocks)
    gap = (index[:, None] - index[None, :] - 1).astype(jnp.float32)
    carry_map = jnp.where(
        gap[None, None] >= 0,
        jnp.exp(-decay_rate[:, :, None, None] * BLK * jnp.maximum(gap, 0.0)),
        0.0,
    )
    entering = jnp.einsum("crab,bcr->acr", carry_map, ends, precision=HIGH)
    tail = (blocks - 1 - index).astype(jnp.float32)
    group_end = jnp.einsum(
        "crb,bcr->cr", jnp.exp(-decay_rate[:, :, None] * BLK * tail), ends, precision=HIGH
    )
    group_decay = jnp.exp(-decay_rate * length)
    incoming = jnp.zeros((chans, modes), jnp.float32)
    for step in range(lax.axis_size("ctx") - 1):
        incoming = shifted(group_decay * incoming + group_end, "ctx", 1)
    lead = jnp.exp(-decay_rate[None] * BLK * index.astype(jnp.float32)[:, None, None])
    entering = entering + lead * incoming[None]
    reach = weight[:, :, None] * powers * pole[:, :, None]
    carried = jnp.einsum("bcr,cri->bic", entering, reach, precision=HIGH)
    conv = (local + carried).reshape(length, chans) + skip_gain * drive
    gated = (query * conv).astype(jnp.bfloat16)
    mixed = jnp.dot(
        lax.all_gather(gated, "tp", axis=1, tiled=True), w_out, preferred_element_type=jnp.float32
    )
    return mixed.astype(jnp.bfloat16)


def solution(mesh):
    in_specs = (
        P("ctx", "tp"),
        P("ctx", None, "tp"),
        P(None, None, "tp"),
        P("tp", None),
        P("tp", None),
        P("tp"),
        P(None, "tp"),
    )
    out_specs = P("ctx", "tp")
    return jax.shard_map(body, mesh=mesh, in_specs=in_specs, out_specs=out_specs, check_vma=False)
```

profile of v0, /device:TPU:96, one launch (start us, length us, event | category | flops | bytes accessed | tf_op | source)
XLA Modules:
  0.0 602.9 jit_solution(1312896963160508286)
XLA Ops:
  7.3 2.6 copy.38
  11.6 179.4 %all-gather.4.cloned.1.call-done = bf16[512,8192]{1,0:T(8,128)(2,1)} async-done(((bf16[512,256]{1,0:T(8,128)(2,1)}), bf16[512,8192]{1,0:T(8,128)(2,1)}) %all-gather.4.cloned.1.call-update) | async-done | bytes 8388624 | tf_op jit(solution)/shard_map/all_gather | solution.py:23
  191.0 136.4 %all-gather.6.cloned.1.call-done = bf16[8192,3,256]{0,2,1:T(8,128)(2,1)} async-done(((bf16[1024,3,256]{0,2,1:T(8,128)(2,1)}), bf16[8192,3,256]{0,2,1:T(8,128)(2,1)}) %all-gather.6.cloned.1.call-update) | async-done | bytes 12582928 | tf_op jit(solution)/shard_map/all_gather | solution.py:24
  327.4 12.8 %convolution_convert_fusion = bf16[512,768]{1,0:T(8,128)(2,1)S(1)} fusion(bf16[512,8192]{1,0:T(8,128)(2,1)} %all-gather.4.cloned.1.call-done, bf16[8192,768]{0,1:T(8,128)(2,1)} %bitcast.50), kind=kOutput, calls=%fused_computation.15 | convolution fusion | flops 6442844160 | bytes 21757952 | tf_op jit(solution)/shard_map/dot_general | solution.py:25
  340.2 1.9 collective-permute-start
  342.2 2.4 rev.3
  348.5 5.6 multiply_reduce_fusion.1
  355.1 1.9 collective-permute-start.1
  357.0 3.1 collective-permute-done.1
  360.1 2.1 collective-permute-start.2
  362.3 9.5 %fusion.2 = f32[256,128,128]{2,0,1:T(8,128)} fusion(s32[128,128]{1,0:T(8,128)S(1)} %iota_subtract_fusion, f32[256,128]{1,0:T(8,128)S(1)} %get-tuple-element.6), kind=kOutput, calls=%fused_computation.3 | convolution fusion | flops 6444548096 | bytes 16973824 | tf_op jit(solution)/shard_map/ck,kij->cij/dot_general | solution.py:45
  371.8 1.9 collective-permute-start.3
  373.8 3.1 collective-permute-done.3
  376.9 1.9 collective-permute-start.4
  378.8 3.1 collective-permute-done.4
  382.0 1.9 collective-permute-start.5
  384.6 2.4 collective-permute-done.5
  387.0 2.1 collective-permute-start.6
  389.1 38.3 %fusion = f32[256,128,4]{1,2,0:T(4,128)S(1)} fusion(f32[4,128,256]{1,0,2:T(4,128)S(1)} %mul.194, f32[256,128,128]{2,0,1:T(8,128)} %fusion.2), kind=kOutput, calls=%fused_computation | convolution fusion | flops 201326592 | bytes 17825792 | tf_op jit(solution)/shard_map/bjc,cij->bic/dot_general | solution.py:47
  427.7 2.1 collective-permute-start.7
  430.9 1.8 collective-permute-done.7
  433.5 4.7 fusion.9
  439.0 149.6 %all-gather.8.cloned.1.call-done = bf16[512,8192]{0,1:T(8,128)(2,1)} async-done(((bf16[512,256]{0,1:T(8,128)(2,1)}), bf16[512,8192]{0,1:T(8,128)(2,1)}) %all-gather.8.cloned.1.call-update) | async-done | bytes 8388624 | tf_op jit(solution)/shard_map/all_gather | solution.py:72
  588.7 7.7 %convolution_convert_fusion.1 = bf16[512,256]{1,0:T(8,128)(2,1)} fusion(bf16[512,8192]{0,1:T(8,128)(2,1)} %all-gather.8.cloned.1.call-done, bf16[8192,256]{1,0:T(8,128)(2,1)} %param.13), kind=kOutput, calls=%fused_computation.17 | convolution fusion | flops 2147614720 | bytes 12845056 | tf_op jit(solution)/shard_map/dot_general | solution.py:71
  (58 shorter events, 11.0 us)
Async XLA Ops:
  6.5 184.5 %all-gather.4.cloned.1.call-start = ((), (), s32[]{:S(2)}) async-start(), calls=%async_computation | async-start | bytes 8650752 | tf_op jit(solution)/shard_map/all_gather | solution.py:23
  7.3 2.8 copy-start
  7.3 2.8 copy-start.4
  7.3 320.1 %all-gather.6.cloned.1.call-start = ((), (), s32[]{:S(2)}) async-start(), calls=%async_computation.1 | async-start | bytes 14155776 | tf_op jit(solution)/shard_map/all_gather | solution.py:24
  10.0 578.7 %all-gather.8.cloned.1.call-start = ((), (), s32[]{:S(2)}) async-start(), calls=%async_computation.2 | async-start | bytes 8650752 | tf_op jit(solution)/shard_map/all_gather | solution.py:72
  10.3 317.1 %copy-start.2 = (f32[256,16]{1,0:T(8,128)}, f32[256,16]{1,0:T(8,128)S(1)}, u32[]{:S(2)}) copy-start(f32[256,16]{1,0:T(8,128)S(1)} %copy.42) | copy-start | bytes 49156
  327.4 14.8 %copy-start.5 = (f32[3,3,256]{2,1,0:T(4,128)S(1)}, f32[3,3,256]{2,1,0:T(4,128)}, u32[]{:S(2)}) copy-start(f32[3,3,256]{2,1,0:T(4,128)} %param.9) | copy-start | bytes 27652
  340.2 2.0 copy-start.1
  340.2 6.0 collective-permute-start
  355.1 5.1 collective-permute-start.1
  360.1 11.7 %collective-permute-start.2 = (f32[256,16]{0,1:T(8,128)S(1)}, f32[256,16]{0,1:T(8,128)S(1)}, u32[]{:S(2)}, u32[]{:S(2)}) collective-permute-start(f32[256,16]{0,1:T(8,128)S(1)} %multiply_add_fusion.5), channel_id=1, source_target_pairs={{0,32},{32,64},{64,96},{96,128},{128,160},{160,192},{192,224},{1,3... | collective-permute-start | bytes 49160 | tf_op jit(solution)/shard_map/ppermute | solution.py:15
  371.8 5.1 collective-permute-start.3
  376.9 5.1 collective-permute-start.4
  382.0 5.1 collective-permute-start.5
  387.0 46.5 %copy-start.3 = (f32[256,16]{1,0:T(8,128)S(1)}, f32[256,16]{1,0:T(8,128)}, u32[]{:S(2)}) copy-start(f32[256,16]{1,0:T(8,128)} %copy-done.2) | copy-start | bytes 49156
  387.0 40.6 %collective-permute-start.6 = (f32[256,16]{0,1:T(8,128)S(1)}, f32[256,16]{0,1:T(8,128)S(1)}, u32[]{:S(2)}, u32[]{:S(2)}) collective-permute-start(f32[256,16]{0,1:T(8,128)S(1)} %multiply_add_fusion.1), channel_id=1, source_target_pairs={{0,32},{32,64},{64,96},{96,128},{128,160},{160,192},{192,224},{1,3... | collective-permute-start | bytes 49160 | tf_op jit(solution)/shard_map/ppermute | solution.py:15
  427.7 5.1 collective-permute-start.7
  433.5 4.7 copy-start.6
Sparse Core Ops, SparseCore 0:
  10.6 180.4 all-gather.3
  192.8 134.5 all-gather.5
  439.2 149.4 all-gather.7
where the time goes:
time: 609 us; the launch traced here: 603 us
  waiting for transfers between devices  480 us (79%)
  matrix products  78.6 us (13%)
  starting transfers between devices  16 us (3%)
  between operations  13.4 us (2%)
  local copies, waits for them, and re-layouts  10.9 us (2%)
    all_gather x1, waiting for transfers between devices, body(): whole = lax.all_gather(tokens, 'tp', axis=1, tiled=True)  179 us
    all_gather x1, waiting for transfers between devices, body(): lax.all_gather(gated, 'tp', axis=1, tiled=True)  150 us
    all_gather x1, waiting for transfers between devices, body(): piece = lax.all_gather(w_in, 'ctx', axis=0, tiled=True)  136 us
    dot_general x1, matrix products, body(): local = jnp.einsum('bjc,cij->bic', split, toeplitz, precision=HIGH)  38.3 us
    ppermute x8, starting transfers between devices, shifted(): return lax.ppermute(array, axis, pairs)  15.9 us
    ppermute x8, waiting for transfers between devices, shifted(): return lax.ppermute(array, axis, pairs)  13.5 us
    dot_general x1, matrix products, body(): jnp.dot(whole, piece.reshape(piece.shape[0], 3 * chans), preferred_elemen...  12.8 us
  transfers between devices with their start and end apart: 11, of which 8 were waited for; matrix products, arithmetic and copies ran while one was open for 10% of the time, Pallas kernels for 0%

commit v1 on v0

v1 whole, which is shorter than its diff:
```python
import functools
import jax
import jax.numpy as jnp
from jax import lax
from jax.experimental import pallas as pl
from jax.experimental.pallas import tpu as pltpu
from jax.sharding import PartitionSpec as P

MESH = pl.DeviceIdType.MESH
BF = jnp.bfloat16
F32 = jnp.float32
SEGS = 8


def place():
    ctx = lax.axis_index("ctx")
    tp = lax.axis_index("tp")
    return tp // 16, ctx // 2, (tp // 4) % 4, tp % 4, ctx % 2


def dev(h, l, y, x, c):
    return (l * 2 + c, h * 16 + y * 4 + x)


def remote(src, dst, send, recv, device):
    return pltpu.make_async_remote_copy(
        src_ref=src, dst_ref=dst, send_sem=send, recv_sem=recv, device_id=device, device_id_type=MESH
    )


class Gather:
    def __init__(self, buf, where, sems):
        self.buf = buf
        self.h, self.l, y, x, self.c = where
        self.a1 = jnp.where(self.c == 0, x, y)
        self.a2 = jnp.where(self.c == 0, y, x)
        self.s1, self.r1, self.s2, self.r2 = sems
        self.half = buf.shape[2] // 2

    def pos(self, d1, d2):
        a1 = (self.a1 + d1 + 4) % 4
        a2 = (self.a2 + d2 + 4) % 4
        return jnp.where(self.c == 0, a2 * 4 + a1, a1 * 4 + a2)

    def at(self, d1, d2):
        a1 = (self.a1 + d1 + 4) % 4
        a2 = (self.a2 + d2 + 4) % 4
        y = jnp.where(self.c == 0, a2, a1)
        x = jnp.where(self.c == 0, a1, a2)
        return dev(self.h, self.l, y, x, self.c)

    def first(self, o, b, d, arriving):
        unit = self.buf.at[b, self.pos(-d if arriving else 0, 0)]
        return remote(unit, unit, self.s1.at[o, d - 1], self.r1.at[o, d - 1], self.at(d, 0))

    def second(self, o, b, d, slot, arriving):
        way = 1 if slot % 2 == 0 else -1
        origin = 0 if slot < 2 else -way
        if arriving:
            origin = origin - way
        unit = self.buf.at[b, self.pos(-d, origin)]
        if slot >= 2:
            unit = unit.at[pl.ds((slot - 2) * self.half, self.half)]
        return remote(unit, unit, self.s2.at[o, d, slot], self.r2.at[o, d, slot], self.at(0, way))

    def start_own(self, o, b):
        for d in (1, 3, 2):
            self.first(o, b, d, False).start()
        self.start_second(o, b, 0)

    def start_second(self, o, b, d):
        for slot in (0, 1):
            self.second(o, b, d, slot, False).start()

    def pass_first(self, o, b):
        for d in (1, 3, 2):
            self.first(o, b, d, True).wait_recv()
            self.start_second(o, b, d)

    def pass_second(self, o, b):
        for d in (0, 1, 3, 2):
            for slot in (0, 1):
                self.second(o, b, d, slot, True).wait_recv()
                self.second(o, b, d, slot + 2, False).start()

    def finish(self, o, b):
        for d in (0, 1, 3, 2):
            for slot in (2, 3):
                self.second(o, b, d, slot, True).wait_recv()

    def wait_sends(self, o, b):
        for d in (1, 3, 2):
            self.first(o, b, d, False).wait_send()
        for d in range(4):
            for slot in range(4):
                self.second(o, b, d, slot, False).wait_send()


def kernel(
    tokens, w_in, taps, decay, residue, skip, w_out, out,
    tok_all, gat_all, w_all, wo, psend, precv, acc, pf, prev, q_s, u_s, y_s, exc, ends, states,
    ps1, pr1, ps2, pr2, ss, rs, ls, es, er,
):
    rows, chans = tokens.shape
    modes = decay.shape[0]
    where = place()
    h, l, y, x, c = where
    half, odd = l // 2, l % 2
    ctx = l * 2 + c
    me = y * 4 + x
    foreign_type = half != h
    z = h * 4 + l

    barrier = pltpu.get_barrier_semaphore()
    partners = []
    for d in range(1, 8):
        zz = (z + d) % 8
        partners.append(dev(zz // 4, zz % 4, y, x, c))
    partners.append(dev(h, l, y, x, 1 - c))
    for d in range(1, 4):
        partners.append(dev(h, l, y, (x + d) % 4, c))
        partners.append(dev(h, l, (y + d) % 4, x, c))
        partners.append(dev(h, (l + d) % 4, y, x, 1 - c))
    for partner in partners:
        pl.semaphore_signal(barrier, inc=1, device_id=partner, device_id_type=MESH)
    pl.semaphore_wait(barrier, len(partners))

    sibling = dev(h, l, y, x, 1 - c)
    across = l + 1 - 2 * odd
    near = dev(h, across, y, x, c)
    mate = dev(h, (l + 2) % 4, y, x, c)
    opposite = dev(1 - h, l, y, x, c)

    to_l = 2 * h + odd
    foreign = tok_all.at[0, me]
    mine = tok_all.at[1, me]
    f0 = remote(tokens, foreign, ss.at[0], rs.at[0], dev(0, to_l, y, x, c))
    f1 = remote(tokens, foreign, ss.at[1], rs.at[0], dev(1, to_l, y, x, c))
    own_far = remote(tokens, mine, ss.at[2], rs.at[1], opposite)
    own_near = pltpu.make_async_copy(tokens, mine, ls.at[0])

    @pl.when(foreign_type)
    def _():
        f0.start()
        f1.start()

    @pl.when(jnp.logical_not(foreign_type))
    def _():
        own_far.start()
        own_near.start()

    mine_q = 2 * odd + c
    near_q = 2 * (1 - odd) + c
    w_near = remote(w_in, w_all.at[mine_q], ss.at[3], rs.at[3], near)
    w_sib = remote(w_in, w_all.at[mine_q], ss.at[4], rs.at[4], sibling)
    w_loc = pltpu.make_async_copy(w_in, w_all.at[mine_q], ls.at[1])
    w_fwd = remote(w_all.at[near_q], w_all.at[near_q], ss.at[5], rs.at[5], sibling)
    wo_loc = pltpu.make_async_copy(w_out, wo, ls.at[2])
    w_near.start()
    w_sib.start()
    w_loc.start()
    wo_loc.start()

    g = Gather(tok_all, where, (ps1.at[0], pr1.at[0], ps2.at[0], pr2.at[0]))
    f0.wait_recv()
    g.start_own(0, 0)
    g.pass_first(0, 0)

    @pl.when(foreign_type)
    def _():
        own_far.wait_recv()

    @pl.when(jnp.logical_not(foreign_type))
    def _():
        own_near.wait()

    g.start_own(1, 1)
    g.pass_second(0, 0)
    remote(w_in, w_all.at[near_q], ss.at[3], rs.at[3], near).wait_recv()
    w_fwd.start()
    g.pass_first(1, 1)
    g.finish(0, 0)
    w_loc.wait()
    remote(w_in, w_all.at[2 * odd + 1 - c], ss.at[4], rs.at[4], sibling).wait_recv()
    remote(w_in, w_all.at[2 * (1 - odd) + 1 - c], ss.at[5], rs.at[5], sibling).wait_recv()

    def multiply(b, n):
        cols = pl.ds(pl.multiple_of(n * chans, chans), chans)
        total = jnp.zeros((rows, chans), F32)
        for pos in range(16):
            block = w_all[pos // 4, pl.ds((pos % 4) * chans, chans), cols]
            total = total + jnp.dot(tok_all[b, pos], block, preferred_element_type=F32)
        return cols, total

    @pl.loop(0, 3)
    def _(n):
        cols, total = multiply(0, n)
        psend[:, cols] = total.astype(BF)

    part = remote(psend, precv, ss.at[6], rs.at[6], mate)
    part.start()
    g.pass_second(1, 1)
    g.finish(1, 1)

    @pl.loop(0, 3)
    def _(n):
        cols, total = multiply(1, n)
        acc[:, cols] = total

    part.wait_recv()
    BLK = 64

    @pl.loop(0, rows // BLK)
    def _(i):
        r = pl.ds(pl.multiple_of(i * BLK, BLK), BLK)
        total = acc[r, :] + precv[r, :].astype(F32)
        pf[pl.ds(pl.multiple_of(i * BLK + 8, 8), BLK), :] = total.astype(BF).astype(F32)

    prev[0] = pf[pl.ds(rows - 8, 16), :].astype(BF)
    later = ctx + 1
    tail = remote(prev.at[0], prev.at[1], ss.at[7], rs.at[7], dev(h, (later // 2) % 4, y, x, later % 2))

    @pl.when(ctx < 7)
    def _():
        tail.start()

    @pl.when(ctx > 0)
    def _():
        tail.wait_recv()
        pf[0:8, :] = prev[1].astype(F32)[8:16]

    @pl.when(ctx == 0)
    def _():
        pf[0:8, :] = jnp.zeros((8, 3 * chans), F32)

    @pl.loop(0, rows // BLK)
    def _(i):
        feats = []
        for s in range(3):
            feat = None
            block = pf[pl.ds(pl.multiple_of(i * BLK, BLK), BLK + 8), pl.ds(s * chans, chans)]
            for k in range(3):
                piece = block[8 - k : 8 - k + BLK]
                term = taps[k, pl.ds(s, 1), :] * piece
                feat = term if feat is None else feat + term
            feats.append(feat)
        r = pl.ds(pl.multiple_of(i * BLK, BLK), BLK)
        q_s[r, :] = feats[0]
        drive = feats[1] * feats[2]
        for lanes in range(chans // 128):
            u_s[lanes, r, :] = drive[:, lanes * 128 : lanes * 128 + 128]

    seg = rows // SEGS
    index = lax.broadcasted_iota(jnp.int32, (SEGS, 128), 0)

    for lanes in range(chans // 128):
        at = pl.ds(lanes * 128, 128)
        rate = [decay[pl.ds(r, 1), at] for r in range(modes)]
        pole = [jnp.broadcast_to(jnp.exp(-d), (SEGS, 128)) for d in rate]

        def grow(step, state):
            row = u_s[lanes, pl.ds(step, SEGS, stride=seg), :]
            return tuple(p * s + row for p, s in zip(pole, state))

        state = lax.fori_loop(0, seg, grow, tuple(jnp.zeros((SEGS, 128), F32) for _ in range(modes)), unroll=2)
        for r in range(modes):
            value = state[r]
            for k in (1, 2, 4):
                moved = jnp.where(index >= k, pltpu.roll(value, k, 0), 0.0)
                value = value + jnp.exp(-(seg * k) * rate[r]) * moved
            ends[pl.ds(r, 1), at] = value[SEGS - 1 : SEGS]
            exc[r, :, at] = jnp.where(index >= 1, pltpu.roll(value, 1, 0), 0.0)

    for d in range(1, 8):
        @pl.when(ctx + d < 8)
        def _():
            to = ctx + d
            remote(ends, states.at[ctx], es.at[d - 1], er.at[d - 1], dev(h, (to // 2) % 4, y, x, to % 2)).start()

    for d in range(1, 8):
        @pl.when(ctx - d >= 0)
        def _():
            remote(ends, states.at[(ctx - d + 8) % 8], es.at[d - 1], er.at[d - 1], sibling).wait_recv()

    group = jnp.exp(-float(rows) * decay[...])
    coming = lax.fori_loop(
        0, ctx, lambda j, value: group * value + states[j], jnp.zeros((modes, chans), F32)
    )
    ends_in = coming

    for lanes in range(chans // 128):
        at = pl.ds(lanes * 128, 128)
        rate = [decay[pl.ds(r, 1), at] for r in range(modes)]
        pole = [jnp.broadcast_to(jnp.exp(-d), (SEGS, 128)) for d in rate]
        weight = []
        state = []
        for r in range(modes):
            single = jnp.exp(-rate[r])
            weight.append(jnp.broadcast_to(residue[pl.ds(r, 1), at] * jnp.sqrt(1.0 - single * single), (SEGS, 128)))
            lead = jnp.exp(-rate[r] * (index * seg).astype(F32))
            state.append(exc[r, :, at] + lead * ends_in[r : r + 1, lanes * 128 : lanes * 128 + 128])

        def emit(step, state):
            row = u_s[lanes, pl.ds(step, SEGS, stride=seg), :]
            state = tuple(p * s + row for p, s in zip(pole, state))
            terms = [w * s for w, s in zip(weight, state)]
            while len(terms) > 1:
                terms = [a + b for a, b in zip(terms[0::2], terms[1::2])]
            y_s[lanes, pl.ds(step, SEGS, stride=seg), :] = terms[0]
            return state

        lax.fori_loop(0, seg, emit, tuple(state), unroll=2)

    @pl.loop(0, rows // BLK)
    def _(i):
        r = pl.ds(pl.multiple_of(i * BLK, BLK), BLK)
        for lanes in range(chans // 128):
            at = pl.ds(lanes * 128, 128)
            conv = y_s[lanes, r, :] + skip[:, at] * u_s[lanes, r, :]
            gat_all[h, me, r, at] = (q_s[r, at] * conv).astype(BF)

    g2 = Gather(gat_all, where, (ps1.at[1], pr1.at[1], ps2.at[1], pr2.at[1]))
    mine_g = gat_all.at[h, me]
    other_g = gat_all.at[1 - h, me]
    swap = remote(mine_g, mine_g, ss.at[8], rs.at[8], opposite)
    swap.start()
    g2.start_own(0, h)
    g2.pass_first(0, h)
    g2.pass_second(0, h)
    remote(other_g, other_g, ss.at[8], rs.at[8], opposite).wait_recv()
    g2.start_own(1, 1 - h)
    g2.finish(0, h)
    wo_loc.wait()

    def project(b):
        total = jnp.zeros((rows, chans), F32)
        for pos in range(16):
            block = wo[pl.ds(pl.multiple_of(b * 16 * chans + pos * chans, chans), chans), :]
            total = total + jnp.dot(gat_all[b, pos], block, preferred_element_type=F32)
        return total

    g2.pass_first(1, 1 - h)
    acc[:, 0:chans] = project(h)
    g2.pass_second(1, 1 - h)
    g2.finish(1, 1 - h)
    out[...] = (acc[:, 0:chans] + project(1 - h)).astype(BF)

    @pl.when(foreign_type)
    def _():
        f0.wait_send()
        f1.wait_send()

    @pl.when(jnp.logical_not(foreign_type))
    def _():
        own_far.wait_send()

    w_near.wait_send()
    w_sib.wait_send()
    w_fwd.wait_send()
    part.wait_send()
    swap.wait_send()

    @pl.when(ctx < 7)
    def _():
        tail.wait_send()

    for d in range(1, 8):
        @pl.when(ctx + d < 8)
        def _():
            remote(ends, states.at[ctx], es.at[d - 1], er.at[d - 1], sibling).wait_send()

    for o in range(2):
        g.wait_sends(o, o)
    g2.wait_sends(0, h)
    g2.wait_sends(1, 1 - h)


def body(tokens, w_in, short_taps, decay_rate, residue, skip_gain, w_out):
    rows, chans = tokens.shape
    depth = w_in.shape[0]
    modes = decay_rate.shape[1]
    vmem = pl.BlockSpec(memory_space=pltpu.VMEM)
    any_ = pl.BlockSpec(memory_space=pl.ANY)
    dma = pltpu.SemaphoreType.DMA
    return pl.pallas_call(
        kernel,
        out_shape=jax.ShapeDtypeStruct((rows, chans), BF),
        in_specs=[vmem, any_, vmem, vmem, vmem, vmem, any_],
        out_specs=vmem,
        scratch_shapes=[
            pltpu.VMEM((2, 16, rows, chans), BF),
            pltpu.VMEM((2, 16, rows, chans), BF),
            pltpu.VMEM((4, depth, 3 * chans), BF),
            pltpu.VMEM(w_out.shape, BF),
            pltpu.VMEM((rows, 3 * chans), BF),
            pltpu.VMEM((rows, 3 * chans), BF),
            pltpu.VMEM((rows, 3 * chans), F32),
            pltpu.VMEM((rows + 8, 3 * chans), F32),
            pltpu.VMEM((2, 16, 3 * chans), BF),
            pltpu.VMEM((rows, chans), F32),
            pltpu.VMEM((chans // 128, rows, 128), F32),
            pltpu.VMEM((chans // 128, rows, 128), F32),
            pltpu.VMEM((modes, SEGS, chans), F32),
            pltpu.VMEM((modes, chans), F32),
            pltpu.VMEM((8, modes, chans), F32),
            dma((2, 2, 3)),
            dma((2, 2, 3)),
            dma((2, 2, 4, 4)),
            dma((2, 2, 4, 4)),
            dma((9,)),
            dma((9,)),
            dma((3,)),
            dma((7,)),
            dma((7,)),
        ],
        compiler_params=pltpu.CompilerParams(collective_id=0, has_side_effects=True, vmem_limit_bytes=56 << 20),
        name="hyena",
    )(
        tokens, w_in.reshape(depth, 3 * chans), short_taps, decay_rate.T, residue.T,
        skip_gain.reshape(1, chans), w_out,
    )


def solution(mesh):
    in_specs = (
        P("ctx", "tp"),
        P("ctx", None, "tp"),
        P(None, None, "tp"),
        P("tp", None),
        P("tp", None),
        P("tp"),
        P(None, "tp"),
    )
    return jax.shard_map(body, mesh=mesh, in_specs=in_specs, out_specs=P("ctx", "tp"), check_vma=False)
```

time: 609 us -> 171 us (0.28); the launches traced: 603 us -> 171 us
  waiting for transfers between devices: 480 us -> 0 us
  Pallas kernels: 0 us -> 166 us
  matrix products: 78.6 us -> 0 us
  starting transfers between devices: 16 us -> 0 us
  between operations: 13.4 us -> 0.02 us
    all_gather x3 -> x0, waiting for transfers between devices: 465 us -> none  [the longest x1 179 us: body(): whole = lax.all_gather(tokens, 'tp', axis=1, tiled=True)]
    pallas_call x0 -> x1, Pallas kernels: none -> 166 us  [body(): pl.pallas_call(kernel, out_shape=jax.ShapeDtypeStruct((rows, chans), BF),...]
    dot_general x6 -> x0, matrix products: 78.6 us -> none  [the longest x1 38.3 us: body(): local = jnp.einsum('bjc,cij->bic', split, toeplitz, precision=HIGH)]
    ppermute x8 -> x0, starting transfers between devices: 15.9 us -> none  [shifted(): return lax.ppermute(array, axis, pairs)]
    ppermute x8 -> x0, waiting for transfers between devices: 13.5 us -> none  [shifted(): return lax.ppermute(array, axis, pairs)]
  transfers between devices with their start and end apart: 11 -> 0, of which waited for: 8 -> 0; matrix products, arithmetic and copies ran while one was open for 10% -> 0% of each run, Pallas kernels for 0% -> 0%
where the time goes in v1:
time: 171 us
  Pallas kernels  166 us (97%)
  local copies, waits for them, and re-layouts  4.97 us (3%)
    pallas_call x1, Pallas kernels, body(): pl.pallas_call(kernel, out_shape=jax.ShapeDtypeStruct((rows, chans), BF),...  166 us

profile of v1, /device:TPU:96, one launch (start us, length us, event | category | flops | bytes accessed | tf_op | source)
XLA Modules:
  0.0 171.2 jit_solution(2507592026308501369)
XLA Ops:
  0.0 1.7 copy.9
  1.7 1.6 copy.10.w_in
  3.3 166.2 %hyena.1 = bf16[512,256]{1,0:T(8,128)(2,1)} custom-call(bf16[512,256]{1,0:T(8,128)(2,1)} %tokens.1, bf16[1024,768]{1,0:T(8,128)(2,1)} %copy.10.w_in, f32[3,3,256]{2,1,0:T(4,128)} %taps.1, f32[16,256]{1,0:T(8,128)} %bitcast.5, f32[16,256]{1,0:T(8,128)} %bitcast.6, f32[1,256]{1,0:T(1,128)} %bitcast.7, bf16[8192,256]{1,0:T(8,128)(2,1)} %w_out.1), custom_call_target="tpu_custom_call" | custom-call | tf_op jit(solution)/shard_map/hyena/pallas_call | solution.py:385
  169.5 1.7 copy.12

commit v2 on v1

v2 whole, which is shorter than its diff:
```python
import functools
import jax
import jax.numpy as jnp
from jax import lax
from jax.experimental import pallas as pl
from jax.experimental.pallas import tpu as pltpu
from jax.sharding import PartitionSpec as P

MESH = pl.DeviceIdType.MESH
BF = jnp.bfloat16
F32 = jnp.float32
SEGS = 8
LANES = 128
HALVES = 2


def place():
    ctx = lax.axis_index("ctx")
    tp = lax.axis_index("tp")
    return tp // 16, ctx // 2, (tp // 4) % 4, tp % 4, ctx % 2


def dev(h, l, y, x, c):
    return (l * 2 + c, h * 16 + y * 4 + x)


def remote(src, dst, send, recv, device):
    return pltpu.make_async_remote_copy(
        src_ref=src, dst_ref=dst, send_sem=send, recv_sem=recv, device_id=device, device_id_type=MESH
    )


class Gather:
    def __init__(self, buf, where, sems):
        self.buf = buf
        self.h, self.l, y, x, self.c = where
        self.a1 = jnp.where(self.c == 0, x, y)
        self.a2 = jnp.where(self.c == 0, y, x)
        self.s1, self.r1, self.s2, self.r2 = sems
        self.half = buf.shape[2] // 2

    def pos(self, d1, d2):
        a1 = (self.a1 + d1 + 4) % 4
        a2 = (self.a2 + d2 + 4) % 4
        return jnp.where(self.c == 0, a2 * 4 + a1, a1 * 4 + a2)

    def at(self, d1, d2):
        a1 = (self.a1 + d1 + 4) % 4
        a2 = (self.a2 + d2 + 4) % 4
        y = jnp.where(self.c == 0, a2, a1)
        x = jnp.where(self.c == 0, a1, a2)
        return dev(self.h, self.l, y, x, self.c)

    def first(self, o, b, d, arriving):
        unit = self.buf.at[b, self.pos(-d if arriving else 0, 0)]
        return remote(unit, unit, self.s1.at[o, d - 1], self.r1.at[o, d - 1], self.at(d, 0))

    def second(self, o, b, d, slot, arriving):
        way = 1 if slot % 2 == 0 else -1
        origin = 0 if slot < 2 else -way
        if arriving:
            origin = origin - way
        unit = self.buf.at[b, self.pos(-d, origin)]
        if slot >= 2:
            unit = unit.at[pl.ds((slot - 2) * self.half, self.half)]
        return remote(unit, unit, self.s2.at[o, d, slot], self.r2.at[o, d, slot], self.at(0, way))

    def start_own(self, o, b):
        for d in (1, 3, 2):
            self.first(o, b, d, False).start()
        self.start_second(o, b, 0)

    def start_second(self, o, b, d):
        for slot in (0, 1):
            self.second(o, b, d, slot, False).start()

    def pass_first(self, o, b):
        for d in (1, 3, 2):
            self.first(o, b, d, True).wait_recv()
            self.start_second(o, b, d)

    def pass_second(self, o, b):
        for d in (0, 1, 3, 2):
            for slot in (0, 1):
                self.second(o, b, d, slot, True).wait_recv()
                self.second(o, b, d, slot + 2, False).start()

    def finish(self, o, b):
        for d in (0, 1, 3, 2):
            for slot in (2, 3):
                self.second(o, b, d, slot, True).wait_recv()

    def wait_sends(self, o, b):
        for d in (1, 3, 2):
            self.first(o, b, d, False).wait_send()
        for d in range(4):
            for slot in range(4):
                self.second(o, b, d, slot, False).wait_send()


def kernel(
    tokens, w_in, taps, decay, residue, skip, w_out, out,
    tok_all, w_all, wx, gat, psend, precv, acc, acc2, osend, orecv, pf, prev, q_s, u_s, y_s, exc, ends, states,
    ps1, pr1, ps2, pr2, ss, rs, ls, es, er, hs, hr, gs, gr, xs, xr, os, orr,
):
    rows, chans = tokens.shape
    modes = decay.shape[0]
    groups = chans // LANES
    wide = 3 * LANES
    where = place()
    h, l, y, x, c = where
    half, odd = l // 2, l % 2
    ctx = l * 2 + c
    me = y * 4 + x
    foreign_type = half != h
    z = h * 4 + l

    barrier = pltpu.get_barrier_semaphore()
    partners = []
    for d in range(1, 8):
        zz = (z + d) % 8
        partners.append(dev(zz // 4, zz % 4, y, x, c))
    partners.append(dev(h, l, y, x, 1 - c))
    for d in range(1, 4):
        partners.append(dev(h, l, y, (x + d) % 4, c))
        partners.append(dev(h, l, (y + d) % 4, x, c))
        partners.append(dev(h, (l + d) % 4, y, x, 1 - c))
    for partner in partners:
        pl.semaphore_signal(barrier, inc=1, device_id=partner, device_id_type=MESH)

    sibling = dev(h, l, y, x, 1 - c)
    across = l + 1 - 2 * odd
    near = dev(h, across, y, x, c)
    mate = dev(h, (l + 2) % 4, y, x, c)
    opposite = dev(1 - h, l, y, x, c)

    to_l = 2 * h + odd
    foreign = tok_all.at[0, me]
    mine = tok_all.at[1, me]
    f0 = remote(tokens, foreign, ss.at[0], rs.at[0], dev(0, to_l, y, x, c))
    f1 = remote(tokens, foreign, ss.at[1], rs.at[0], dev(1, to_l, y, x, c))
    own_far = remote(tokens, mine, ss.at[2], rs.at[1], opposite)
    own_near = pltpu.make_async_copy(tokens, mine, ls.at[0])

    mine_q = 2 * odd + c
    near_q = 2 * (1 - odd) + c

    def w_piece(g):
        return w_in.at[:, :, pl.ds(g * LANES, LANES)]

    def w_near(g, q):
        return remote(w_piece(g), w_all.at[q, g], hs.at[0, g], hr.at[0, g], near)

    def w_sib(g, q):
        return remote(w_piece(g), w_all.at[q, g], hs.at[1, g], hr.at[1, g], sibling)

    def w_fwd(g, q):
        return remote(w_all.at[q, g], w_all.at[q, g], ss.at[3 + g], rs.at[3 + g], sibling)

    def w_loc(g):
        return pltpu.make_async_copy(w_piece(g), w_all.at[mine_q, g], ls.at[1 + g])

    def o_piece(to_x, g):
        return w_out.at[:, to_x, g]

    o_loc = [pltpu.make_async_copy(o_piece(x, g), wx.at[x, g], ls.at[7 + g]) for g in range(groups)]

    def o_send(d, arriving):
        to_x = (x + d) % 4
        slot = wx.at[(x - d + 4) % 4 if arriving else x, c]
        return remote(o_piece(to_x, c), slot, ss.at[4 + d], rs.at[4 + d], dev(h, l, y, to_x, c))

    def o_fwd(d, arriving):
        slot = wx.at[(x - d + 4) % 4, 1 - c if arriving else c]
        return remote(slot, slot, ss.at[7 + d], rs.at[7 + d], sibling)

    @pl.when(jnp.logical_not(foreign_type))
    def _():
        own_near.start()

    for g in range(groups):
        w_loc(g).start()
    for copy in o_loc:
        copy.start()

    pl.semaphore_wait(barrier, len(partners))

    @pl.when(foreign_type)
    def _():
        f0.start()
        f1.start()

    def start_near(g):
        w_near(g, mine_q).start()

    def pass_near(g):
        w_near(g, near_q).wait_recv()
        w_fwd(g, near_q).start()

    def have_weights(g):
        w_loc(g).wait()
        w_sib(g, 2 * odd + 1 - c).wait_recv()
        w_fwd(g, 2 * (1 - odd) + 1 - c).wait_recv()

    start_near(0)
    for g in range(groups):
        w_sib(g, mine_q).start()

    def multiply(b, g, r):
        total = jnp.zeros((rows // 2, wide), F32)
        for pos in range(16):
            here = pl.ds((pos % 4) * chans, chans)
            block = jnp.concatenate([w_all[pos // 4, g, s, here, :] for s in range(3)], axis=1)
            total = total + jnp.dot(tok_all[b, pos, r, :], block, preferred_element_type=F32)
        return total

    def halves(body):
        @pl.loop(0, 2)
        def _(i):
            body(pl.ds(pl.multiple_of(i * (rows // 2), rows // 2), rows // 2))

    def part(g):
        return remote(psend.at[g], precv.at[g], ss.at[11 + g], rs.at[11 + g], mate)

    def foreign_part(g):
        def tile(r):
            psend[g, r, :] = multiply(0, g, r).astype(BF)

        halves(tile)
        part(g).start()

    def own_part(g):
        def tile(r):
            acc[g, r, :] = multiply(1, g, r)

        halves(tile)

    t = Gather(tok_all, where, (ps1, pr1, ps2, pr2))
    f0.wait_recv()
    t.start_own(0, 0)

    @pl.when(jnp.logical_not(foreign_type))
    def _():
        own_far.start()

    t.pass_first(0, 0)
    start_near(1)
    t.pass_second(0, 0)

    @pl.when(foreign_type)
    def _():
        own_far.wait_recv()

    @pl.when(jnp.logical_not(foreign_type))
    def _():
        own_near.wait()

    t.start_own(1, 1)
    pass_near(0)
    t.finish(0, 0)
    have_weights(0)
    foreign_part(0)
    t.pass_first(1, 1)
    pass_near(1)
    have_weights(1)
    foreign_part(1)
    t.pass_second(1, 1)
    for d in (1, 3, 2):
        o_send(d, False).start()
    t.finish(1, 1)

    BLK = 64
    seg = rows // SEGS
    index = lax.broadcasted_iota(jnp.int32, (SEGS, LANES), 0)
    later = ctx + 1
    before = lax.max(ctx, 1) - 1

    def tail(g):
        return remote(
            prev.at[g, 0], prev.at[g, 1], ss.at[13 + g], rs.at[13 + g], dev(h, (later // 2) % 4, y, x, later % 2)
        )

    def project_rows(g):
        part(g).wait_recv()

        @pl.loop(0, rows // BLK)
        def _(i):
            r = pl.ds(pl.multiple_of(i * BLK, BLK), BLK)
            total = acc[g, r, :] + precv[g, r, :].astype(F32)
            pf[g, pl.ds(pl.multiple_of(i * BLK + 8, 8), BLK), :] = total.astype(BF).astype(F32)

        prev[g, 0] = pf[g, pl.ds(rows - 8, 16), :].astype(BF)

        @pl.when(ctx < 7)
        def _():
            tail(g).start()

    def features(g):
        at = pl.ds(g * LANES, LANES)

        def some(i):
            feats = []
            for s in range(3):
                feat = None
                block = pf[g, pl.ds(pl.multiple_of(i * BLK, BLK), BLK + 8), pl.ds(s * LANES, LANES)]
                for k in range(3):
                    piece = block[8 - k : 8 - k + BLK]
                    term = taps[k, pl.ds(s, 1), at] * piece
                    feat = term if feat is None else feat + term
                feats.append(feat)
            r = pl.ds(pl.multiple_of(i * BLK, BLK), BLK)
            q_s[g, r, :] = feats[0]
            u_s[g, r, :] = feats[1] * feats[2]

        pl.loop(1, rows // BLK)(some)

        @pl.when(ctx > 0)
        def _():
            tail(g).wait_recv()
            pf[g, 0:8, :] = prev[g, 1].astype(F32)[8:16]

        @pl.when(ctx == 0)
        def _():
            pf[g, 0:8, :] = jnp.zeros((8, wide), F32)

        pl.loop(0, 1)(some)

    def rates(g):
        return [decay[pl.ds(r, 1), pl.ds(g * LANES, LANES)] for r in range(modes)]

    def state_copy(g, d, to, slot):
        return remote(ends.at[g], states.at[g, slot], es.at[g, d - 1], er.at[g, d - 1], to)

    def scan_ends(g):
        rate = rates(g)
        pole = [jnp.broadcast_to(jnp.exp(-d), (SEGS, LANES)) for d in rate]

        def grow(step, state):
            row = u_s[g, pl.ds(step, SEGS, stride=seg), :]
            return tuple(p * s + row for p, s in zip(pole, state))

        state = lax.fori_loop(0, seg, grow, tuple(jnp.zeros((SEGS, LANES), F32) for _ in range(modes)), unroll=2)
        for r in range(modes):
            value = state[r]
            for k in (1, 2, 4):
                moved = jnp.where(index >= k, pltpu.roll(value, k, 0), 0.0)
                value = value + jnp.exp(-(seg * k) * rate[r]) * moved
            ends[g, pl.ds(r, 1), :] = value[SEGS - 1 : SEGS]
            exc[g, r] = jnp.where(index >= 1, pltpu.roll(value, 1, 0), 0.0)
        for d in range(1, 8):
            @pl.when(ctx + d < 8)
            def _():
                to = ctx + d
                state_copy(g, d, dev(h, (to // 2) % 4, y, x, to % 2), ctx).start()

    def scan_out(g):
        for d in range(1, 8):
            @pl.when(ctx - d >= 0)
            def _():
                state_copy(g, d, sibling, (ctx - d + 8) % 8).wait_recv()

        group = jnp.exp(-float(rows) * decay[:, pl.ds(g * LANES, LANES)])
        coming = lax.fori_loop(
            0, ctx, lambda j, value: group * value + states[g, j], jnp.zeros((modes, LANES), F32)
        )
        rate = rates(g)
        pole = [jnp.broadcast_to(jnp.exp(-d), (SEGS, LANES)) for d in rate]
        weight = []
        state = []
        for r in range(modes):
            single = jnp.exp(-rate[r])
            scale = residue[pl.ds(r, 1), pl.ds(g * LANES, LANES)] * jnp.sqrt(1.0 - single * single)
            weight.append(jnp.broadcast_to(scale, (SEGS, LANES)))
            lead = jnp.exp(-rate[r] * (index * seg).astype(F32))
            state.append(exc[g, r] + lead * coming[r : r + 1])

        def emit(step, state):
            row = u_s[g, pl.ds(step, SEGS, stride=seg), :]
            state = tuple(p * s + row for p, s in zip(pole, state))
            terms = [w * s for w, s in zip(weight, state)]
            while len(terms) > 1:
                terms = [a + b for a, b in zip(terms[0::2], terms[1::2])]
            y_s[g, pl.ds(step, SEGS, stride=seg), :] = terms[0]
            return state

        lax.fori_loop(0, seg, emit, tuple(state), unroll=2)

        count = rows // BLK // HALVES
        for p in range(HALVES):
            @pl.loop(p * count, (p + 1) * count)
            def _(i):
                r = pl.ds(pl.multiple_of(i * BLK, BLK), BLK)
                conv = y_s[g, r, :] + skip[:, pl.ds(g * LANES, LANES)] * u_s[g, r, :]
                gat[g, y, r, mine_h] = (q_s[g, r, :] * conv).astype(BF)

            swap(g, p, False).start()
            for d in (1, 3, 2):
                along(g, 0, p, d, False).start()

    mine_h = pl.ds(pl.multiple_of(h * LANES, LANES), LANES)
    other_h = pl.ds(pl.multiple_of((1 - h) * LANES, LANES), LANES)
    step = rows // HALVES

    def swap(g, p, arriving):
        unit = gat.at[g, y, pl.ds(p * step, step), other_h if arriving else mine_h]
        return remote(unit, unit, xs.at[g, p], xr.at[g, p], opposite)

    def along(g, o, p, d, arriving):
        from_y = (y - d + 4) % 4 if arriving else y
        unit = gat.at[g, from_y, pl.ds(p * step, step), mine_h if o == 0 else other_h]
        return remote(unit, unit, gs.at[g, o, p, d - 1], gr.at[g, o, p, d - 1], dev(h, l, (y + d) % 4, x, c))

    def pass_gated(g, p):
        swap(g, p, True).wait_recv()
        for d in (1, 3, 2):
            along(g, 1, p, d, False).start()

    def have_gated(g, p):
        for o in range(2):
            for d in (1, 3, 2):
                along(g, o, p, d, True).wait_recv()

    def output(g, to_x, p):
        r = pl.ds(p * step, step)
        total = jnp.zeros((step, chans), F32)
        for k in range(4):
            block = jnp.concatenate([wx[to_x, g, k], wx[to_x, g, 4 + k]], axis=0)
            total = total + jnp.dot(gat[g, k, r, :], block, preferred_element_type=F32)
        return total

    def result(d, p, arriving):
        r = pl.ds(p * step, step)
        return remote(
            osend.at[d - 1, r], orecv.at[d - 1, r], os.at[d - 1, p], orr.at[d - 1, p], dev(h, l, y, (x + d) % 4, c)
        )

    own_part(0)
    project_rows(0)
    own_part(1)
    features(0)
    scan_ends(0)
    scan_out(0)
    project_rows(1)
    features(1)
    scan_ends(1)
    for p in range(HALVES):
        pass_gated(0, p)
    scan_out(1)
    for copy in o_loc:
        copy.wait()
    for d in (1, 3, 2):
        o_send(d, True).wait_recv()
        o_fwd(d, False).start()
    for d in (1, 3, 2):
        o_fwd(d, True).wait_recv()
    for p in range(HALVES):
        have_gated(0, p)
    for p in range(HALVES):
        if p == 1:
            pass_gated(1, 0)
        r = pl.ds(p * step, step)
        for d in range(4):
            acc2[d, r, :] = output(0, (x + d) % 4, p)
    for p in range(1, HALVES):
        pass_gated(1, p)
    for p in range(HALVES):
        r = pl.ds(p * step, step)
        have_gated(1, p)
        for d in (2, 1, 3):
            osend[d - 1, r, :] = (acc2[d, r, :] + output(1, (x + d) % 4, p)).astype(BF)
            result(d, p, False).start()
    for p in range(HALVES):
        r = pl.ds(p * step, step)
        acc2[0, r, :] = acc2[0, r, :] + output(1, x, p)
    for p in range(HALVES):
        r = pl.ds(p * step, step)
        for d in (2, 1, 3):
            result(d, p, True).wait_recv()
        out[r, :] = (
            acc2[0, r, :] + orecv[0, r, :].astype(F32) + orecv[1, r, :].astype(F32) + orecv[2, r, :].astype(F32)
        ).astype(BF)

    @pl.when(foreign_type)
    def _():
        f0.wait_send()
        f1.wait_send()

    @pl.when(jnp.logical_not(foreign_type))
    def _():
        own_far.wait_send()

    for g in range(groups):
        w_near(g, mine_q).wait_send()
        w_sib(g, mine_q).wait_send()
        w_fwd(g, near_q).wait_send()
        part(g).wait_send()
        for p in range(HALVES):
            swap(g, p, False).wait_send()
            for o in range(2):
                for d in (1, 3, 2):
                    along(g, o, p, d, False).wait_send()

        @pl.when(ctx < 7)
        def _():
            tail(g).wait_send()

        for d in range(1, 8):
            @pl.when(ctx + d < 8)
            def _():
                state_copy(g, d, sibling, ctx).wait_send()

    for d in (1, 3, 2):
        o_send(d, False).wait_send()
        o_fwd(d, False).wait_send()
        for p in range(HALVES):
            result(d, p, False).wait_send()
    for o in range(2):
        t.wait_sends(o, o)


def body(tokens, w_in, short_taps, decay_rate, residue, skip_gain, w_out):
    rows, chans = tokens.shape
    depth = w_in.shape[0]
    modes = decay_rate.shape[1]
    groups = chans // LANES
    vmem = pl.BlockSpec(memory_space=pltpu.VMEM)
    any_ = pl.BlockSpec(memory_space=pl.ANY)
    dma = pltpu.SemaphoreType.DMA
    return pl.pallas_call(
        kernel,
        out_shape=jax.ShapeDtypeStruct((rows, chans), BF),
        in_specs=[vmem, any_, vmem, vmem, vmem, vmem, any_],
        out_specs=vmem,
        scratch_shapes=[
            pltpu.VMEM((2, 16, rows, chans), BF),
            pltpu.VMEM((4, groups, 3, depth, LANES), BF),
            pltpu.VMEM((4, groups, 8, LANES, chans), BF),
            pltpu.VMEM((groups, 4, rows, 2 * LANES), BF),
            pltpu.VMEM((groups, rows, 3 * LANES), BF),
            pltpu.VMEM((groups, rows, 3 * LANES), BF),
            pltpu.VMEM((groups, rows, 3 * LANES), F32),
            pltpu.VMEM((4, rows, chans), F32),
            pltpu.VMEM((3, rows, chans), BF),
            pltpu.VMEM((3, rows, chans), BF),
            pltpu.VMEM((groups, rows + 8, 3 * LANES), F32),
            pltpu.VMEM((groups, 2, 16, 3 * LANES), BF),
            pltpu.VMEM((groups, rows, LANES), F32),
            pltpu.VMEM((groups, rows, LANES), F32),
            pltpu.VMEM((groups, rows, LANES), F32),
            pltpu.VMEM((groups, modes, SEGS, LANES), F32),
            pltpu.VMEM((groups, modes, LANES), F32),
            pltpu.VMEM((groups, 8, modes, LANES), F32),
            dma((2, 3)),
            dma((2, 3)),
            dma((2, 4, 4)),
            dma((2, 4, 4)),
            dma((21,)),
            dma((21,)),
            dma((9,)),
            dma((groups, 7)),
            dma((groups, 7)),
            dma((2, groups)),
            dma((2, groups)),
            dma((groups, 2, HALVES, 3)),
            dma((groups, 2, HALVES, 3)),
            dma((groups, HALVES)),
            dma((groups, HALVES)),
            dma((3, HALVES)),
            dma((3, HALVES)),
        ],
        compiler_params=pltpu.CompilerParams(collective_id=0, has_side_effects=True, vmem_limit_bytes=56 << 20),
        name="hyena",
    )(
        tokens, jnp.transpose(w_in, (1, 0, 2)), short_taps, decay_rate.T, residue.T,
        skip_gain.reshape(1, chans), w_out.reshape(8, 4, groups, LANES, chans),
    )


def solution(mesh):
    in_specs = (
        P("ctx", "tp"),
        P("ctx", None, "tp"),
        P(None, None, "tp"),
        P("tp", None),
        P("tp", None),
        P("tp"),
        P(None, "tp"),
    )
    return jax.shard_map(body, mesh=mesh, in_specs=in_specs, out_specs=P("ctx", "tp"), check_vma=False)
```

time: 171 us -> 139 us (0.81)
  Pallas kernels: 166 us -> 137 us
  local copies, waits for them, and re-layouts: 4.97 us -> 1.67 us
    pallas_call x1, Pallas kernels: 166 us -> 137 us  [body(): pl.pallas_call(kernel, out_shape=jax.ShapeDtypeStruct((rows, chans), BF),...]
where the time goes in v2:
time: 139 us
  Pallas kernels  137 us (99%)
  local copies, waits for them, and re-layouts  1.67 us (1%)
    pallas_call x1, Pallas kernels, body(): pl.pallas_call(kernel, out_shape=jax.ShapeDtypeStruct((rows, chans), BF),...  137 us

profile of v2, /device:TPU:96, one launch (start us, length us, event | category | flops | bytes accessed | tf_op | source)
XLA Modules:
  0.0 138.6 jit_solution(15402906506184148902)
XLA Ops:
  0.0 136.9 %hyena.1 = bf16[512,256]{1,0:T(8,128)(2,1)} custom-call(bf16[512,256]{1,0:T(8,128)(2,1)} %tokens.1, bf16[3,1024,256]{2,1,0:T(8,128)(2,1)} %bitcast.6, f32[3,3,256]{2,1,0:T(4,128)} %taps.1, f32[16,256]{1,0:T(8,128)} %bitcast.7, f32[16,256]{1,0:T(8,128)} %bitcast.8, f32[1,256]{1,0:T(1,128)} %bitcast.9, bf16[8,4,2,128,256]{4,3,2,1,0:T(8,128)(2,1)} %bitcast.5), custom_call_target="tpu_custom_call" | custom-call | tf_op jit(solution)/shard_map/hyena/pallas_call | solution.py:529
  136.9 1.7 %copy.9 = bf16[512,256]{1,0:T(8,128)(2,1)} copy(bf16[512,256]{1,0:T(8,128)(2,1)} %hyena.1) | data formatting | bytes 524288

commit v3 on v2

--- a/solution.py
+++ b/solution.py
@@ -37,12 +37,17 @@
         self.a1 = jnp.where(self.c == 0, x, y)
         self.a2 = jnp.where(self.c == 0, y, x)
         self.s1, self.r1, self.s2, self.r2 = sems
-        self.half = buf.shape[2] // 2
-
-    def pos(self, d1, d2):
+        self.step = buf.shape[2] // HALVES
+
+    def unit(self, o, d1, d2, quarter=None):
         a1 = (self.a1 + d1 + 4) % 4
         a2 = (self.a2 + d2 + 4) % 4
-        return jnp.where(self.c == 0, a2 * 4 + a1, a1 * 4 + a2)
+        pos = jnp.where(self.c == 0, a2 * 4 + a1, a1 * 4 + a2)
+        if quarter is None:
+            rows = pl.ds((o % HALVES) * self.step, self.step)
+        else:
+            rows = pl.ds((o % HALVES) * self.step + quarter * (self.step // 2), self.step // 2)
+        return self.buf.at[o // HALVES, pos, rows]
 
     def at(self, d1, d2):
         a1 = (self.a1 + d1 + 4) % 4
@@ -51,57 +56,55 @@
         x = jnp.where(self.c == 0, a1, a2)
         return dev(self.h, self.l, y, x, self.c)
 
-    def first(self, o, b, d, arriving):
-        unit = self.buf.at[b, self.pos(-d if arriving else 0, 0)]
+    def first(self, o, d, arriving):
+        unit = self.unit(o, -d if arriving else 0, 0)
         return remote(unit, unit, self.s1.at[o, d - 1], self.r1.at[o, d - 1], self.at(d, 0))
 
-    def second(self, o, b, d, slot, arriving):
+    def second(self, o, d, slot, arriving):
         way = 1 if slot % 2 == 0 else -1
         origin = 0 if slot < 2 else -way
         if arriving:
             origin = origin - way
-        unit = self.buf.at[b, self.pos(-d, origin)]
-        if slot >= 2:
-            unit = unit.at[pl.ds((slot - 2) * self.half, self.half)]
+        unit = self.unit(o, -d, origin, None if slot < 2 else slot - 2)
         return remote(unit, unit, self.s2.at[o, d, slot], self.r2.at[o, d, slot], self.at(0, way))
 
-    def start_own(self, o, b):
+    def start_own(self, o):
         for d in (1, 3, 2):
-            self.first(o, b, d, False).start()
-        self.start_second(o, b, 0)
-
-    def start_second(self, o, b, d):
+            self.first(o, d, False).start()
+        self.start_second(o, 0)
+
+    def start_second(self, o, d):
         for slot in (0, 1):
-            self.second(o, b, d, slot, False).start()
-
-    def pass_first(self, o, b):
+            self.second(o, d, slot, False).start()
+
+    def pass_first(self, o):
         for d in (1, 3, 2):
-            self.first(o, b, d, True).wait_recv()
-            self.start_second(o, b, d)
-
-    def pass_second(self, o, b):
+            self.first(o, d, True).wait_recv()
+            self.start_second(o, d)
+
+    def pass_second(self, o):
         for d in (0, 1, 3, 2):
             for slot in (0, 1):
-                self.second(o, b, d, slot, True).wait_recv()
-                self.second(o, b, d, slot + 2, False).start()
-
-    def finish(self, o, b):
+                self.second(o, d, slot, True).wait_recv()
+                self.second(o, d, slot + 2, False).start()
+
+    def finish(self, o):
         for d in (0, 1, 3, 2):
             for slot in (2, 3):
-                self.second(o, b, d, slot, True).wait_recv()
-
-    def wait_sends(self, o, b):
+                self.second(o, d, slot, True).wait_recv()
+
+    def wait_sends(self, o):
         for d in (1, 3, 2):
-            self.first(o, b, d, False).wait_send()
+            self.first(o, d, False).wait_send()
         for d in range(4):
             for slot in range(4):
-                self.second(o, b, d, slot, False).wait_send()
+                self.second(o, d, slot, False).wait_send()
 
 
 def kernel(
     tokens, w_in, taps, decay, residue, skip, w_out, out,
     tok_all, w_all, wx, gat, psend, precv, acc, acc2, osend, orecv, pf, prev, q_s, u_s, y_s, exc, ends, states,
-    ps1, pr1, ps2, pr2, ss, rs, ls, es, er, hs, hr, gs, gr, xs, xr, os, orr,
+    ps1, pr1, ps2, pr2, ss, rs, ls, es, er, hs, hr, gs, gr, xs, xr, os, orr, fs, fr, qs, qr,
 ):
     rows, chans = tokens.shape
     modes = decay.shape[0]
@@ -135,12 +138,15 @@
     opposite = dev(1 - h, l, y, x, c)
 
     to_l = 2 * h + odd
-    foreign = tok_all.at[0, me]
-    mine = tok_all.at[1, me]
-    f0 = remote(tokens, foreign, ss.at[0], rs.at[0], dev(0, to_l, y, x, c))
-    f1 = remote(tokens, foreign, ss.at[1], rs.at[0], dev(1, to_l, y, x, c))
-    own_far = remote(tokens, mine, ss.at[2], rs.at[1], opposite)
-    own_near = pltpu.make_async_copy(tokens, mine, ls.at[0])
+    step = rows // HALVES
+
+    def token_copy(kind, p):
+        r = pl.ds(p * step, step)
+        place = tok_all.at[0 if kind < 2 else 1, me, r]
+        to = opposite if kind == 2 else dev(kind, to_l, y, x, c)
+        return remote(tokens.at[r], place, fs.at[kind, p], fr.at[kind // 2, p], to)
+
+    own_near = pltpu.make_async_copy(tokens, tok_all.at[1, me], ls.at[0])
 
     mine_q = 2 * odd + c
     near_q = 2 * (1 - odd) + c
@@ -187,8 +193,9 @@
 
     @pl.when(foreign_type)
     def _():
-        f0.start()
-        f1.start()
+        for p in range(HALVES):
+            token_copy(0, p).start()
+            token_copy(1, p).start()
 
     def start_near(g):
         w_near(g, mine_q).start()
@@ -206,68 +213,76 @@
     for g in range(groups):
         w_sib(g, mine_q).start()
 
-    def multiply(b, g, r):
-        total = jnp.zeros((rows // 2, wide), F32)
+    def multiply(b, g, p):
+        r = pl.ds(p * step, step)
+        total = jnp.zeros((step, wide), F32)
         for pos in range(16):
             here = pl.ds((pos % 4) * chans, chans)
             block = jnp.concatenate([w_all[pos // 4, g, s, here, :] for s in range(3)], axis=1)
             total = total + jnp.dot(tok_all[b, pos, r, :], block, preferred_element_type=F32)
         return total
 
-    def halves(body):
-        @pl.loop(0, 2)
-        def _(i):
-            body(pl.ds(pl.multiple_of(i * (rows // 2), rows // 2), rows // 2))
-
-    def part(g):
-        return remote(psend.at[g], precv.at[g], ss.at[11 + g], rs.at[11 + g], mate)
-
-    def foreign_part(g):
-        def tile(r):
-            psend[g, r, :] = multiply(0, g, r).astype(BF)
-
-        halves(tile)
-        part(g).start()
-
-    def own_part(g):
-        def tile(r):
-            acc[g, r, :] = multiply(1, g, r)
-
-        halves(tile)
+    def part(g, p):
+        r = pl.ds(p * step, step)
+        return remote(psend.at[g, r], precv.at[g, r], qs.at[g, p], qr.at[g, p], mate)
+
+    def foreign_part(g, p):
+        psend[g, pl.ds(p * step, step), :] = multiply(0, g, p).astype(BF)
+        part(g, p).start()
+
+    def own_part(g, p):
+        acc[g, pl.ds(p * step, step), :] = multiply(1, g, p)
+
+    def have_own():
+        @pl.when(foreign_type)
+        def _():
+            for p in range(HALVES):
+                token_copy(2, p).wait_recv()
+
+        @pl.when(jnp.logical_not(foreign_type))
+        def _():
+            own_near.wait()
 
     t = Gather(tok_all, where, (ps1, pr1, ps2, pr2))
-    f0.wait_recv()
-    t.start_own(0, 0)
+    token_copy(0, 0).wait_recv()
+    t.start_own(0)
+    token_copy(0, 1).wait_recv()
 
     @pl.when(jnp.logical_not(foreign_type))
     def _():
-        own_far.start()
-
-    t.pass_first(0, 0)
+        for p in range(HALVES):
+            token_copy(2, p).start()
+
+    t.pass_first(0)
+    t.start_own(1)
+    t.pass_second(0)
     start_near(1)
-    t.pass_second(0, 0)
-
-    @pl.when(foreign_type)
-    def _():
-        own_far.wait_recv()
-
-    @pl.when(jnp.logical_not(foreign_type))
-    def _():
-        own_near.wait()
-
-    t.start_own(1, 1)
+    t.pass_first(1)
+    t.finish(0)
     pass_near(0)
-    t.finish(0, 0)
+    t.pass_second(1)
+    have_own()
+    t.start_own(2)
     have_weights(0)
-    foreign_part(0)
-    t.pass_first(1, 1)
+    foreign_part(0, 0)
+    t.finish(1)
+    foreign_part(0, 1)
+    t.pass_first(2)
+    t.start_own(3)
+    t.pass_second(2)
+    t.pass_first(3)
     pass_near(1)
     have_weights(1)
-    foreign_part(1)
-    t.pass_second(1, 1)
+    foreign_part(1, 0)
+    foreign_part(1, 1)
+    t.pass_second(3)
     for d in (1, 3, 2):
         o_send(d, False).start()
-    t.finish(1, 1)
+    t.finish(2)
+    own_part(0, 0)
+    own_part(1, 0)
+    t.finish(3)
+    own_part(0, 1)
 
     BLK = 64
     seg = rows // SEGS
@@ -281,7 +296,8 @@
         )
 
     def project_rows(g):
-        part(g).wait_recv()
+        for p in range(HALVES):
+            part(g, p).wait_recv()
 
         @pl.loop(0, rows // BLK)
         def _(i):
@@ -385,40 +401,49 @@
 
         lax.fori_loop(0, seg, emit, tuple(state), unroll=2)
 
-        count = rows // BLK // HALVES
-        for p in range(HALVES):
-            @pl.loop(p * count, (p + 1) * count)
-            def _(i):
-                r = pl.ds(pl.multiple_of(i * BLK, BLK), BLK)
-                conv = y_s[g, r, :] + skip[:, pl.ds(g * LANES, LANES)] * u_s[g, r, :]
-                gat[g, y, r, mine_h] = (q_s[g, r, :] * conv).astype(BF)
-
-            swap(g, p, False).start()
-            for d in (1, 3, 2):
-                along(g, 0, p, d, False).start()
+        @pl.loop(0, rows // BLK)
+        def _(i):
+            r = pl.ds(pl.multiple_of(i * BLK, BLK), BLK)
+            conv = y_s[g, r, :] + skip[:, pl.ds(g * LANES, LANES)] * u_s[g, r, :]
+            gat[g, y, r, mine_h] = (q_s[g, r, :] * conv).astype(BF)
 
     mine_h = pl.ds(pl.multiple_of(h * LANES, LANES), LANES)
     other_h = pl.ds(pl.multiple_of((1 - h) * LANES, LANES), LANES)
-    step = rows // HALVES
-
     def swap(g, p, arriving):
         unit = gat.at[g, y, pl.ds(p * step, step), other_h if arriving else mine_h]
         return remote(unit, unit, xs.at[g, p], xr.at[g, p], opposite)
 
-    def along(g, o, p, d, arriving):
-        from_y = (y - d + 4) % 4 if arriving else y
-        unit = gat.at[g, from_y, pl.ds(p * step, step), mine_h if o == 0 else other_h]
-        return remote(unit, unit, gs.at[g, o, p, d - 1], gr.at[g, o, p, d - 1], dev(h, l, (y + d) % 4, x, c))
-
-    def pass_gated(g, p):
+    def along(g, o, p, slot, arriving):
+        way = 1 if slot % 2 == 0 else -1
+        origin = 0 if slot < 2 else -way
+        if arriving:
+            origin = origin - way
+        if slot < 2:
+            r = pl.ds(p * step, step)
+        else:
+            r = pl.ds(p * step + (slot - 2) * (step // 2), step // 2)
+        unit = gat.at[g, (y + origin + 4) % 4, r, mine_h if o == 0 else other_h]
+        return remote(unit, unit, gs.at[g, o, p, slot], gr.at[g, o, p, slot], dev(h, l, (y + way + 4) % 4, x, c))
+
+    def send_gated(g, p):
+        swap(g, p, False).start()
+        for slot in (0, 1):
+            along(g, 0, p, slot, False).start()
+
+    def pass_swap(g, p):
         swap(g, p, True).wait_recv()
-        for d in (1, 3, 2):
-            along(g, 1, p, d, False).start()
+        for slot in (0, 1):
+            along(g, 1, p, slot, False).start()
+
+    def pass_along(g, o, p):
+        for slot in (0, 1):
+            along(g, o, p, slot, True).wait_recv()
+            along(g, o, p, slot + 2, False).start()
 
     def have_gated(g, p):
         for o in range(2):
-            for d in (1, 3, 2):
-                along(g, o, p, d, True).wait_recv()
+            for slot in (2, 3):
+                along(g, o, p, slot, True).wait_recv()
 
     def output(g, to_x, p):
         r = pl.ds(p * step, step)
@@ -434,71 +459,85 @@
             osend.at[d - 1, r], orecv.at[d - 1, r], os.at[d - 1, p], orr.at[d - 1, p], dev(h, l, y, (x + d) % 4, c)
         )
 
-    own_part(0)
     project_rows(0)
-    own_part(1)
+    own_part(1, 1)
+    project_rows(1)
     features(0)
     scan_ends(0)
-    scan_out(0)
-    project_rows(1)
     features(1)
     scan_ends(1)
-    for p in range(HALVES):
-        pass_gated(0, p)
-    scan_out(1)
+    for o in range(2 * HALVES):
+        t.wait_sends(o)
     for copy in o_loc:
         copy.wait()
+    scan_out(0)
+    send_gated(0, 0)
+    scan_out(1)
+    send_gated(1, 0)
+    send_gated(0, 1)
+    send_gated(1, 1)
+    pass_along(0, 0, 0)
+    pass_along(1, 0, 0)
+    pass_along(0, 0, 1)
+    pass_swap(0, 0)
+    pass_along(1, 0, 1)
+    pass_swap(1, 0)
+    pass_swap(0, 1)
+    pass_swap(1, 1)
     for d in (1, 3, 2):
         o_send(d, True).wait_recv()
         o_fwd(d, False).start()
+    pass_along(0, 1, 0)
+    pass_along(1, 1, 0)
+    pass_along(0, 1, 1)
     for d in (1, 3, 2):
         o_fwd(d, True).wait_recv()
+    have_gated(0, 0)
+    have_gated(1, 0)
+
+    def send_results(p):
+        r = pl.ds(p * step, step)
+        for d in (2, 1, 3):
+            to_x = (x + d) % 4
+            osend[d - 1, r, :] = (output(0, to_x, p) + output(1, to_x, p)).astype(BF)
+            result(d, p, False).start()
+
+    send_results(0)
+    pass_along(1, 1, 1)
+    have_gated(0, 1)
+    have_gated(1, 1)
+    send_results(1)
     for p in range(HALVES):
-        have_gated(0, p)
-    for p in range(HALVES):
-        if p == 1:
-            pass_gated(1, 0)
-        r = pl.ds(p * step, step)
-        for d in range(4):
-            acc2[d, r, :] = output(0, (x + d) % 4, p)
-    for p in range(1, HALVES):
-        pass_gated(1, p)
-    for p in range(HALVES):
-        r = pl.ds(p * step, step)
-        have_gated(1, p)
-        for d in (2, 1, 3):
-            osend[d - 1, r, :] = (acc2[d, r, :] + output(1, (x + d) % 4, p)).astype(BF)
-            result(d, p, False).start()
-    for p in range(HALVES):
-        r = pl.ds(p * step, step)
-        acc2[0, r, :] = acc2[0, r, :] + output(1, x, p)
+        acc2[pl.ds(p * step, step), :] = output(0, x, p) + output(1, x, p)
     for p in range(HALVES):
         r = pl.ds(p * step, step)
         for d in (2, 1, 3):
             result(d, p, True).wait_recv()
         out[r, :] = (
-            acc2[0, r, :] + orecv[0, r, :].astype(F32) + orecv[1, r, :].astype(F32) + orecv[2, r, :].astype(F32)
+            acc2[r, :] + orecv[0, r, :].astype(F32) + orecv[1, r, :].astype(F32) + orecv[2, r, :].astype(F32)
         ).astype(BF)
 
     @pl.when(foreign_type)
     def _():
-        f0.wait_send()
-        f1.wait_send()
+        for p in range(HALVES):
+            token_copy(0, p).wait_send()
+            token_copy(1, p).wait_send()
 
     @pl.when(jnp.logical_not(foreign_type))
     def _():
-        own_far.wait_send()
+        for p in range(HALVES):
+            token_copy(2, p).wait_send()
 
     for g in range(groups):
         w_near(g, mine_q).wait_send()
         w_sib(g, mine_q).wait_send()
         w_fwd(g, near_q).wait_send()
-        part(g).wait_send()
         for p in range(HALVES):
+            part(g, p).wait_send()
             swap(g, p, False).wait_send()
             for o in range(2):
-                for d in (1, 3, 2):
-                    along(g, o, p, d, False).wait_send()
+                for slot in range(4):
+                    along(g, o, p, slot, False).wait_send()
 
         @pl.when(ctx < 7)
         def _():
@@ -514,9 +553,6 @@
         o_fwd(d, False).wait_send()
         for p in range(HALVES):
             result(d, p, False).wait_send()
-    for o in range(2):
-        t.wait_sends(o, o)
-
 
 def body(tokens, w_in, short_taps, decay_rate, residue, skip_gain, w_out):
     rows, chans = tokens.shape
@@ -539,7 +575,7 @@
             pltpu.VMEM((groups, rows, 3 * LANES), BF),
             pltpu.VMEM((groups, rows, 3 * LANES), BF),
             pltpu.VMEM((groups, rows, 3 * LANES), F32),
-            pltpu.VMEM((4, rows, chans), F32),
+            pltpu.VMEM((rows, chans), F32),
             pltpu.VMEM((3, rows, chans), BF),
             pltpu.VMEM((3, rows, chans), BF),
             pltpu.VMEM((groups, rows + 8, 3 * LANES), F32),
@@ -550,10 +586,10 @@
             pltpu.VMEM((groups, modes, SEGS, LANES), F32),
             pltpu.VMEM((groups, modes, LANES), F32),
             pltpu.VMEM((groups, 8, modes, LANES), F32),
-            dma((2, 3)),
-            dma((2, 3)),
-            dma((2, 4, 4)),
-            dma((2, 4, 4)),
+            dma((2 * HALVES, 3)),
+            dma((2 * HALVES, 3)),
+            dma((2 * HALVES, 4, 4)),
+            dma((2 * HALVES, 4, 4)),
             dma((21,)),
             dma((21,)),
             dma((9,)),
@@ -561,12 +597,16 @@
             dma((groups, 7)),
             dma((2, groups)),
             dma((2, groups)),
-            dma((groups, 2, HALVES, 3)),
-            dma((groups, 2, HALVES, 3)),
+            dma((groups, 2, HALVES, 4)),
+            dma((groups, 2, HALVES, 4)),
             dma((groups, HALVES)),
             dma((groups, HALVES)),
             dma((3, HALVES)),
             dma((3, HALVES)),
+            dma((3, HALVES)),
+            dma((2, HALVES)),
+            dma((groups, HALVES)),
+            dma((groups, HALVES)),
         ],
         compiler_params=pltpu.CompilerParams(collective_id=0, has_side_effects=True, vmem_limit_bytes=56 << 20),
         name="hyena",

time: 139 us -> 130 us (0.935)
  Pallas kernels: 137 us -> 128 us
    pallas_call x1, Pallas kernels: 137 us -> 128 us  [body(): pl.pallas_call(kernel, out_shape=jax.ShapeDtypeStruct((rows, chans), BF),...]
where the time goes in v3:
time: 130 us
  Pallas kernels  128 us (98%)
  local copies, waits for them, and re-layouts  1.67 us (1%)
    pallas_call x1, Pallas kernels, body(): pl.pallas_call(kernel, out_shape=jax.ShapeDtypeStruct((rows, chans), BF),...  128 us

profile of v3, /device:TPU:96, one launch (start us, length us, event | category | flops | bytes accessed | tf_op | source)
XLA Modules:
  0.0 129.6 jit_solution(2646379109172700249)
XLA Ops:
  0.0 127.9 %hyena.1 = bf16[512,256]{1,0:T(8,128)(2,1)} custom-call(bf16[512,256]{1,0:T(8,128)(2,1)} %tokens.1, bf16[3,1024,256]{2,1,0:T(8,128)(2,1)} %bitcast.6, f32[3,3,256]{2,1,0:T(4,128)} %taps.1, f32[16,256]{1,0:T(8,128)} %bitcast.7, f32[16,256]{1,0:T(8,128)} %bitcast.8, f32[1,256]{1,0:T(1,128)} %bitcast.9, bf16[8,4,2,128,256]{4,3,2,1,0:T(8,128)(2,1)} %bitcast.5), custom_call_target="tpu_custom_call" | custom-call | tf_op jit(solution)/shard_map/hyena/pallas_call | solution.py:565
  127.9 1.7 %copy.9 = bf16[512,256]{1,0:T(8,128)(2,1)} copy(bf16[512,256]{1,0:T(8,128)(2,1)} %hyena.1) | data formatting | bytes 524288

commit v4 on v3

--- a/solution.py
+++ b/solution.py
@@ -58,7 +58,7 @@
 
     def first(self, o, d, arriving):
         unit = self.unit(o, -d if arriving else 0, 0)
-        return remote(unit, unit, self.s1.at[o, d - 1], self.r1.at[o, d - 1], self.at(d, 0))
+        return remote(unit, unit, self.s1.at[o % 2, d - 1], self.r1.at[o, d - 1], self.at(d, 0))
 
     def second(self, o, d, slot, arriving):
         way = 1 if slot % 2 == 0 else -1
@@ -66,7 +66,7 @@
         if arriving:
             origin = origin - way
         unit = self.unit(o, -d, origin, None if slot < 2 else slot - 2)
-        return remote(unit, unit, self.s2.at[o, d, slot], self.r2.at[o, d, slot], self.at(0, way))
+        return remote(unit, unit, self.s2.at[o % 2, d, slot], self.r2.at[o, d, slot], self.at(0, way))
 
     def start_own(self, o):
         for d in (1, 3, 2):
@@ -104,7 +104,7 @@
 def kernel(
     tokens, w_in, taps, decay, residue, skip, w_out, out,
     tok_all, w_all, wx, gat, psend, precv, acc, acc2, osend, orecv, pf, prev, q_s, u_s, y_s, exc, ends, states,
-    ps1, pr1, ps2, pr2, ss, rs, ls, es, er, hs, hr, gs, gr, xs, xr, os, orr, fs, fr, qs, qr,
+    ps1, pr1, ps2, pr2, ss, rs, ls, es, er, hs, hr, gr, xs, xr, orr, fs, fr, qs, qr, bs, br,
 ):
     rows, chans = tokens.shape
     modes = decay.shape[0]
@@ -157,6 +157,13 @@
     def w_near(g, q):
         return remote(w_piece(g), w_all.at[q, g], hs.at[0, g], hr.at[0, g], near)
 
+    def w_near_b(s, q):
+        return remote(w_in.at[s, :, pl.ds(LANES, LANES)], w_all.at[q, 1, s], bs.at[0, s], br.at[0, s], near)
+
+    def w_fwd_b(s, q):
+        block = w_all.at[q, 1, s]
+        return remote(block, block, bs.at[1, s], br.at[1, s], sibling)
+
     def w_sib(g, q):
         return remote(w_piece(g), w_all.at[q, g], hs.at[1, g], hr.at[1, g], sibling)
 
@@ -197,19 +204,20 @@
             token_copy(0, p).start()
             token_copy(1, p).start()
 
-    def start_near(g):
-        w_near(g, mine_q).start()
-
-    def pass_near(g):
-        w_near(g, near_q).wait_recv()
-        w_fwd(g, near_q).start()
+    def pass_near():
+        w_near(0, near_q).wait_recv()
+        w_fwd(0, near_q).start()
+
+    def pass_near_b(s):
+        w_near_b(s, near_q).wait_recv()
+        w_fwd_b(s, near_q).start()
 
     def have_weights(g):
         w_loc(g).wait()
         w_sib(g, 2 * odd + 1 - c).wait_recv()
-        w_fwd(g, 2 * (1 - odd) + 1 - c).wait_recv()
-
-    start_near(0)
+
+    far_q = 2 * (1 - odd) + 1 - c
+    w_near(0, mine_q).start()
     for g in range(groups):
         w_sib(g, mine_q).start()
 
@@ -222,13 +230,28 @@
             total = total + jnp.dot(tok_all[b, pos, r, :], block, preferred_element_type=F32)
         return total
 
-    def part(g, p):
+    def part(p):
         r = pl.ds(p * step, step)
-        return remote(psend.at[g, r], precv.at[g, r], qs.at[g, p], qr.at[g, p], mate)
-
-    def foreign_part(g, p):
-        psend[g, pl.ds(p * step, step), :] = multiply(0, g, p).astype(BF)
-        part(g, p).start()
+        return remote(psend.at[0, r], precv.at[0, r], qs.at[p], qr.at[p], mate)
+
+    def foreign_part(p):
+        psend[0, pl.ds(p * step, step), :] = multiply(0, 0, p).astype(BF)
+        part(p).start()
+
+    def part_b(s):
+        cols = pl.ds(s * LANES, LANES)
+        return remote(psend.at[1, :, cols], precv.at[1, :, cols], bs.at[2, s], br.at[2, s], mate)
+
+    def foreign_part_b(s):
+        w_fwd_b(s, far_q).wait_recv()
+        for p in range(HALVES):
+            r = pl.ds(p * step, step)
+            total = jnp.zeros((step, LANES), F32)
+            for pos in range(16):
+                block = w_all[pos // 4, 1, s, pl.ds((pos % 4) * chans, chans), :]
+                total = total + jnp.dot(tok_all[0, pos, r, :], block, preferred_element_type=F32)
+            psend[1, r, pl.ds(s * LANES, LANES)] = total.astype(BF)
+        part_b(s).start()
 
     def own_part(g, p):
         acc[g, pl.ds(p * step, step), :] = multiply(1, g, p)
@@ -256,30 +279,38 @@
     t.pass_first(0)
     t.start_own(1)
     t.pass_second(0)
-    start_near(1)
+    w_near_b(0, mine_q).start()
     t.pass_first(1)
     t.finish(0)
-    pass_near(0)
+    pass_near()
+    w_near_b(1, mine_q).start()
     t.pass_second(1)
     have_own()
+    t.wait_sends(0)
     t.start_own(2)
     have_weights(0)
-    foreign_part(0, 0)
+    w_fwd(0, far_q).wait_recv()
+    foreign_part(0)
     t.finish(1)
-    foreign_part(0, 1)
+    w_near_b(2, mine_q).start()
+    foreign_part(1)
     t.pass_first(2)
+    t.wait_sends(1)
     t.start_own(3)
+    pass_near_b(0)
     t.pass_second(2)
+    have_weights(1)
+    foreign_part_b(0)
     t.pass_first(3)
-    pass_near(1)
-    have_weights(1)
-    foreign_part(1, 0)
-    foreign_part(1, 1)
+    pass_near_b(1)
+    foreign_part_b(1)
+    t.finish(2)
+    own_part(0, 0)
     t.pass_second(3)
+    pass_near_b(2)
+    foreign_part_b(2)
     for d in (1, 3, 2):
         o_send(d, False).start()
-    t.finish(2)
-    own_part(0, 0)
     own_part(1, 0)
     t.finish(3)
     own_part(0, 1)
@@ -296,8 +327,12 @@
         )
 
     def project_rows(g):
-        for p in range(HALVES):
-            part(g, p).wait_recv()
+        if g == 0:
+            for p in range(HALVES):
+                part(p).wait_recv()
+        else:
+            for s in range(3):
+                part_b(s).wait_recv()
 
         @pl.loop(0, rows // BLK)
         def _(i):
@@ -423,7 +458,7 @@
         else:
             r = pl.ds(p * step + (slot - 2) * (step // 2), step // 2)
         unit = gat.at[g, (y + origin + 4) % 4, r, mine_h if o == 0 else other_h]
-        return remote(unit, unit, gs.at[g, o, p, slot], gr.at[g, o, p, slot], dev(h, l, (y + way + 4) % 4, x, c))
+        return remote(unit, unit, ps2.at[g, o * 2 + p, slot], gr.at[g, o, p, slot], dev(h, l, (y + way + 4) % 4, x, c))
 
     def send_gated(g, p):
         swap(g, p, False).start()
@@ -456,7 +491,7 @@
     def result(d, p, arriving):
         r = pl.ds(p * step, step)
         return remote(
-            osend.at[d - 1, r], orecv.at[d - 1, r], os.at[d - 1, p], orr.at[d - 1, p], dev(h, l, y, (x + d) % 4, c)
+            osend.at[d - 1, r], orecv.at[d - 1, r], ps1.at[p, d - 1], orr.at[d - 1, p], dev(h, l, y, (x + d) % 4, c)
         )
 
     project_rows(0)
@@ -466,8 +501,8 @@
     scan_ends(0)
     features(1)
     scan_ends(1)
-    for o in range(2 * HALVES):
-        t.wait_sends(o)
+    t.wait_sends(2)
+    t.wait_sends(3)
     for copy in o_loc:
         copy.wait()
     scan_out(0)
@@ -490,6 +525,7 @@
     pass_along(0, 1, 0)
     pass_along(1, 1, 0)
     pass_along(0, 1, 1)
+    pass_along(1, 1, 1)
     for d in (1, 3, 2):
         o_fwd(d, True).wait_recv()
     have_gated(0, 0)
@@ -503,7 +539,6 @@
             result(d, p, False).start()
 
     send_results(0)
-    pass_along(1, 1, 1)
     have_gated(0, 1)
     have_gated(1, 1)
     send_results(1)
@@ -529,11 +564,8 @@
             token_copy(2, p).wait_send()
 
     for g in range(groups):
-        w_near(g, mine_q).wait_send()
         w_sib(g, mine_q).wait_send()
-        w_fwd(g, near_q).wait_send()
         for p in range(HALVES):
-            part(g, p).wait_send()
             swap(g, p, False).wait_send()
             for o in range(2):
                 for slot in range(4):
@@ -548,6 +580,14 @@
             def _():
                 state_copy(g, d, sibling, ctx).wait_send()
 
+    w_near(0, mine_q).wait_send()
+    w_fwd(0, near_q).wait_send()
+    for p in range(HALVES):
+        part(p).wait_send()
+    for s in range(3):
+        w_near_b(s, mine_q).wait_send()
+        w_fwd_b(s, near_q).wait_send()
+        part_b(s).wait_send()
     for d in (1, 3, 2):
         o_send(d, False).wait_send()
         o_fwd(d, False).wait_send()
@@ -586,9 +626,9 @@
             pltpu.VMEM((groups, modes, SEGS, LANES), F32),
             pltpu.VMEM((groups, modes, LANES), F32),
             pltpu.VMEM((groups, 8, modes, LANES), F32),
+            dma((2, 3)),
             dma((2 * HALVES, 3)),
-            dma((2 * HALVES, 3)),
-            dma((2 * HALVES, 4, 4)),
+            dma((2, 4, 4)),
             dma((2 * HALVES, 4, 4)),
             dma((21,)),
             dma((21,)),
@@ -598,15 +638,15 @@
             dma((2, groups)),
             dma((2, groups)),
             dma((groups, 2, HALVES, 4)),
-            dma((groups, 2, HALVES, 4)),
             dma((groups, HALVES)),
             dma((groups, HALVES)),
             dma((3, HALVES)),
             dma((3, HALVES)),
-            dma((3, HALVES)),
             dma((2, HALVES)),
-            dma((groups, HALVES)),
-            dma((groups, HALVES)),
+            dma((HALVES,)),
+            dma((HALVES,)),
+            dma((3, 3)),
+            dma((3, 3)),
         ],
         compiler_params=pltpu.CompilerParams(collective_id=0, has_side_effects=True, vmem_limit_bytes=56 << 20),
         name="hyena",

time: 130 us -> 126 us (0.969)
  Pallas kernels: 128 us -> 124 us
    pallas_call x1, Pallas kernels: 128 us -> 124 us  [body(): pl.pallas_call(kernel, out_shape=jax.ShapeDtypeStruct((rows, chans), BF),...]
where the time goes in v4:
time: 126 us
  Pallas kernels  124 us (98%)
  local copies, waits for them, and re-layouts  1.67 us (1%)
    pallas_call x1, Pallas kernels, body(): pl.pallas_call(kernel, out_shape=jax.ShapeDtypeStruct((rows, chans), BF),...  124 us

profile of v4, /device:TPU:96, one launch (start us, length us, event | category | flops | bytes accessed | tf_op | source)
XLA Modules:
  0.0 125.6 jit_solution(4213439782530009022)
XLA Ops:
  0.0 123.9 %hyena.1 = bf16[512,256]{1,0:T(8,128)(2,1)} custom-call(bf16[512,256]{1,0:T(8,128)(2,1)} %tokens.1, bf16[3,1024,256]{2,1,0:T(8,128)(2,1)} %bitcast.6, f32[3,3,256]{2,1,0:T(4,128)} %taps.1, f32[16,256]{1,0:T(8,128)} %bitcast.7, f32[16,256]{1,0:T(8,128)} %bitcast.8, f32[1,256]{1,0:T(1,128)} %bitcast.9, bf16[8,4,2,128,256]{4,3,2,1,0:T(8,128)(2,1)} %bitcast.5), custom_call_target="tpu_custom_call" | custom-call | tf_op jit(solution)/shard_map/hyena/pallas_call | solution.py:605
  123.9 1.7 %copy.9 = bf16[512,256]{1,0:T(8,128)(2,1)} copy(bf16[512,256]{1,0:T(8,128)(2,1)} %hyena.1) | data formatting | bytes 524288

commit v5 on v4

--- a/solution.py
+++ b/solution.py
@@ -304,13 +304,13 @@
     t.pass_first(3)
     pass_near_b(1)
     foreign_part_b(1)
-    t.finish(2)
-    own_part(0, 0)
     t.pass_second(3)
     pass_near_b(2)
     foreign_part_b(2)
     for d in (1, 3, 2):
         o_send(d, False).start()
+    t.finish(2)
+    own_part(0, 0)
     own_part(1, 0)
     t.finish(3)
     own_part(0, 1)

time: 126 us -> 124 us (0.984)
  Pallas kernels: 124 us -> 122 us
    pallas_call x1, Pallas kernels: 124 us -> 122 us  [body(): pl.pallas_call(kernel, out_shape=jax.ShapeDtypeStruct((rows, chans), BF),...]
where the time goes in v5:
time: 124 us
  Pallas kernels  122 us (98%)
  local copies, waits for them, and re-layouts  1.67 us (1%)
    pallas_call x1, Pallas kernels, body(): pl.pallas_call(kernel, out_shape=jax.ShapeDtypeStruct((rows, chans), BF),...  122 us

profile of v5, /device:TPU:96, one launch (start us, length us, event | category | flops | bytes accessed | tf_op | source)
XLA Modules:
  0.0 124.0 jit_solution(5095482606493189185)
XLA Ops:
  0.0 122.3 %hyena.1 = bf16[512,256]{1,0:T(8,128)(2,1)} custom-call(bf16[512,256]{1,0:T(8,128)(2,1)} %tokens.1, bf16[3,1024,256]{2,1,0:T(8,128)(2,1)} %bitcast.6, f32[3,3,256]{2,1,0:T(4,128)} %taps.1, f32[16,256]{1,0:T(8,128)} %bitcast.7, f32[16,256]{1,0:T(8,128)} %bitcast.8, f32[1,256]{1,0:T(1,128)} %bitcast.9, bf16[8,4,2,128,256]{4,3,2,1,0:T(8,128)(2,1)} %bitcast.5), custom_call_target="tpu_custom_call" | custom-call | tf_op jit(solution)/shard_map/hyena/pallas_call | solution.py:605
  122.3 1.7 %copy.9 = bf16[512,256]{1,0:T(8,128)(2,1)} copy(bf16[512,256]{1,0:T(8,128)(2,1)} %hyena.1) | data formatting | bytes 524288
